TPU v7x, 32 devices: a whole 2x2x4 slice. The times are simulated.
32 devices in a mesh: aa: 4 (over z), col: 2 (over core), pb: 4 (over y, x).
Axes of the slice: x: 2, y: 2, z: 4, core: 2. Of those that a mesh axis runs over, the one named last changes fastest.
Arguments:
- b_ac: bfloat16 [1536, 512, 1024], P('pb', 'aa', 'col'), may hold values from -6 to 6
- b_oc: bfloat16 [1536, 32, 1024], P('pb', None, 'col'), may hold values from -6 to 6
- t1: bfloat16 [32, 512], P(None, 'aa'), may hold values from -0.59765625 to 0.59765625
- f_bd: bfloat16 [1536, 256], P('pb'), may hold values from -0.15625 to 0.15625
- t2: bfloat16 [512, 32768], P('aa', ('col', 'pb')), may hold values from -0.046875 to 0.046875
Outputs:
- residual: float32 [512, 4096], P(('col', 'pb'), 'aa')
All inputs are finite; a program needn't handle non-finite values.
Results may differ from a plain program's by a relative error of at most 0.0041.
Values may be sent and summed in bfloat16 or wider, within the bound.
A program may use at most 256 MiB of HBM per device.

v0:
```python
import jax
import jax.numpy as jnp
from jax import lax
from jax.sharding import PartitionSpec as P

BB = 8
DB = 32
LANES = 128


def shards(b_ac, b_oc, t1, f_bd, t2):
    pairs, width = t2.shape
    c_width = width // DB
    if c_width % LANES or pairs % LANES:
        return narrow_shards(b_ac, b_oc, t1, f_bd, t2)
    amplitudes = t2.reshape(pairs, c_width, DB).transpose(0, 2, 1)
    gathered = lax.all_gather(amplitudes, ("aa", "pb"), axis=0)
    n_aa, n_pb = lax.axis_size("aa"), lax.axis_size("pb")
    gathered = gathered.reshape(n_aa, n_pb, pairs, DB, c_width)
    correction = jnp.einsum("ka,qkc->qac", t1, b_oc, preferred_element_type=jnp.float32)
    dressed = (b_ac - correction).astype(jnp.bfloat16)
    ladder = jnp.einsum("qac,qn->anc", dressed, f_bd, preferred_element_type=jnp.float32)
    ladder = ladder.astype(jnp.bfloat16)
    ladder = ladder.reshape(ladder.shape[0], BB, DB, n_pb, c_width)
    partial_sums = jnp.einsum(
        "xpidc,abdpc->xiab", gathered, ladder, preferred_element_type=jnp.float32
    )
    partial_sums = partial_sums.reshape(n_aa * pairs, -1)
    return lax.psum_scatter(partial_sums, ("col", "pb"), scatter_dimension=0, tiled=True)


def narrow_shards(b_ac, b_oc, t1, f_bd, t2):
    correction = jnp.einsum("ka,qkc->qac", t1, b_oc, preferred_element_type=jnp.float32)
    dressed = (b_ac - correction).astype(jnp.bfloat16)
    regrouped = lax.all_to_all(dressed, "pb", split_axis=2, concat_axis=0, tiled=True)
    a_width = regrouped.shape[1]
    c_width = regrouped.shape[2]
    flat_factors = regrouped.reshape(regrouped.shape[0], a_width * c_width)
    contract_rows = (((0,), (0,)), ((), ()))
    factor_all = lax.all_gather(f_bd, "pb", axis=0, tiled=True)
    ladder = lax.dot_general(
        flat_factors, factor_all, contract_rows, preferred_element_type=jnp.float32
    )
    ladder = ladder.astype(jnp.bfloat16)
    ladder = (
        ladder.reshape(a_width, c_width, BB, DB)
        .transpose(0, 2, 1, 3)
        .reshape(a_width * BB, c_width * DB)
    )
    partial_sums = lax.dot_general(
        lax.all_gather(t2, "aa", axis=0, tiled=True),
        ladder,
        (((1,), (1,)), ((), ())),
        preferred_element_type=jnp.float32,
    )
    return lax.psum_scatter(partial_sums, ("col", "pb"), scatter_dimension=0, tiled=True)


def solution(mesh):
    placed = (
        P("pb", "aa", "col"),
        P("pb", None, "col"),
        P(None, "aa"),
        P("pb", None),
        P("aa", ("col", "pb")),
    )
    return jax.shard_map(
        shards, mesh=mesh, in_specs=placed, out_specs=P(("col", "pb"), "aa"), check_vma=False
    )
```

profile of v0, /device:TPU:0, one launch (start us, length us, event | category | flops | bytes accessed | tf_op | source)
XLA Modules:
  0.0 362.2 jit_solution(12081262053090636870)
XLA Ops:
  6.5 0.0 copy-start
  6.5 0.0 all-gather.3.cloned.1.call-start
  6.5 2.3 copy.19
  8.9 0.0 all-gather.3.cloned.1.call-update
  8.9 0.0 copy-start.2
  8.9 0.0 reduce-scatter.4.cloned.1.call-start
  9.0 64.7 %copy.16 = bf16[384,128,512]{1,2,0:T(8,128)(2,1)} copy(bf16[384,128,512]{2,1,0:T(8,128)(2,1)} %param.5) | data formatting | bytes 100663296 | tf_op args[0]
  73.7 0.0 copy-done.2
  73.7 37.5 %fusion = bf16[384,128,512]{1,2,0:T(8,128)(2,1)} fusion(bf16[384,128,512]{1,2,0:T(8,128)(2,1)} %copy.16, bf16[384,32,512]{2,1,0:T(8,128)(2,1)} %param.6, bf16[32,128]{1,0:T(8,128)(2,1)S(1)} %copy-done.2), kind=kOutput, calls=%fused_computation.1 | convolution fusion | flops 1686110208 | bytes 113254400 | tf_op jit(solution)/shard_map/ka,qkc->qac/dot_general | solution.py:20
  111.2 69.6 %copy.17 = bf16[384,128,512]{0,2,1:T(8,128)(2,1)} copy(bf16[384,128,512]{1,2,0:T(8,128)(2,1)} %fusion) | data formatting | bytes 100663296 | tf_op jit(solution)/shard_map/convert_element_type | solution.py:21
  180.8 0.0 copy-done
  180.8 32.1 %convert_bitcast_fusion = bf16[128,256,512]{1,2,0:T(8,128)(2,1)} fusion(bf16[384,128,512]{0,2,1:T(8,128)(2,1)} %copy.17, bf16[384,256]{1,0:T(8,128)(2,1)S(1)} %copy-done), kind=kOutput, calls=%fused_computation.2 | convolution fusion | flops 12901679104 | bytes 84082688 | tf_op jit(solution)/shard_map/qac,qn->anc/dot_general | solution.py:22
  213.0 47.1 %copy.18 = bf16[128,256,512]{0,2,1:T(8,128)(2,1)} copy(bf16[128,256,512]{1,2,0:T(8,128)(2,1)} %convert_bitcast_fusion) | data formatting | bytes 67108864 | tf_op jit(solution)/shard_map/convert_element_type | solution.py:23
  260.1 2.3 all-gather.3.cloned.1.call-done
  262.4 25.5 %copy.20 = bf16[2048,32,128]{2,1,0:T(8,128)(2,1)} copy(bf16[2048,32,128]{0,1,2:T(8,128)(2,1)} %all-gather.3.cloned.1.call-done) | data formatting | bytes 33554432 | tf_op jit(solution)/shard_map/all_gather | solution.py:17
  288.0 0.0 copy-start.1
  288.0 23.5 %fusion.4 = f32[4,128,128,8]{1,2,0,3:T(8,128)S(1)} fusion(bf16[128,8,32,4,128,1]{0,4,3,2,5,1:T(8,128)(2,1)} %bitcast.45, bf16[4,4,128,32,128]{4,3,2,1,0:T(8,128)(2,1)} %bitcast.46), kind=kOutput, calls=%fused_computation.8 | convolution fusion | flops 17179869184 | bytes 52428800 | tf_op jit(solution)/shard_map/xpidc,abdpc->xiab/dot_general | solution.py:25
  311.5 1.4 copy.41
  312.8 0.2 copy.40
  313.0 1.9 copy.29
  314.9 0.0 reduce-scatter.4.cloned.1.call-update
  314.9 40.4 %reduce-scatter.4.cloned.1.call-done = f32[64,1024]{1,0:T(8,128)} async-done(((f32[512,1024]{1,0:T(8,128)}), f32[64,1024]{1,0:T(8,128)}) %reduce-scatter.4.cloned.1.call-update) | async-done | bytes 262160 | tf_op jit(solution)/shard_map/reduce_scatter | solution.py:29
  355.3 0.0 copy-done.1
Async XLA Ops:
  6.5 174.3 %copy-start = (bf16[384,256]{1,0:T(8,128)(2,1)S(1)}, bf16[384,256]{1,0:T(8,128)(2,1)}, u32[]{:S(2)}) copy-start(bf16[384,256]{1,0:T(8,128)(2,1)} %param.8) | copy-start | bytes 589828
  6.5 255.9 %all-gather.3.cloned.1.call-start = ((), (), s32[]{:S(2)}) async-start(), calls=%async_computation.1 | async-start | bytes 17825792 | tf_op jit(solution)/shard_map/all_gather | solution.py:17
  8.9 64.8 %copy-start.2 = (bf16[32,128]{1,0:T(8,128)(2,1)S(1)}, bf16[32,128]{1,0:T(8,128)(2,1)}, u32[]{:S(2)}) copy-start(bf16[32,128]{1,0:T(8,128)(2,1)} %param.7) | copy-start | bytes 24580
  8.9 346.4 %reduce-scatter.4.cloned.1.call-start = ((), (), s32[]{:S(2)}) async-start(), calls=%async_computation.2 | async-start | bytes 2359296 | tf_op jit(solution)/shard_map/reduce_scatter | solution.py:29
  288.0 67.4 %copy-start.1 = (bf16[384,256]{1,0:T(8,128)(2,1)S(1)}, bf16[384,256]{1,0:T(8,128)(2,1)}, u32[]{:S(2)}) copy-start(bf16[384,256]{1,0:T(8,128)(2,1)} %param.8) | copy-start | bytes 589828
Sparse Core Ops, SparseCore 0:
  10.1 252.3 all-gather.2
  315.0 40.2 reduce-scatter.3
where the time goes:
time: 368 us; the launch traced here: 362 us
  local copies, waits for them, and re-layouts  213 us (58%)
  matrix products  93.2 us (25%)
  waiting for transfers between devices  42.8 us (12%)
  between operations  13.4 us (4%)
    convert_element_type x1, local copies, waits for them, and re-layouts, shards(): dressed = (b_ac - correction).astype(jnp.bfloat16)  69.6 us
    unnamed x10, local copies, waits for them, and re-layouts  69.1 us
    convert_element_type x1, local copies, waits for them, and re-layouts, shards(): ladder = ladder.astype(jnp.bfloat16)  47.1 us
    reduce_scatter x1, waiting for transfers between devices, shards(): lax.psum_scatter(partial_sums, ('col', 'pb'), scatter_dimension=0, tiled=...  40.4 us
    dot_general x1, matrix products, shards(): jnp.einsum('ka,qkc->qac', t1, b_oc, preferred_element_type=jnp.float32)  37.5 us
    dot_general x1, matrix products, shards(): jnp.einsum('qac,qn->anc', dressed, f_bd, preferred_element_type=jnp.float32)  32.1 us
    all_gather x1, local copies, waits for them, and re-layouts, shards(): gathered = lax.all_gather(amplitudes, ('aa', 'pb'), axis=0)  25.5 us
    dot_general x1, matrix products, shards(): jnp.einsum('xpidc,abdpc->xiab', gathered, ladder, preferred_element_type=...  23.5 us
  transfers between devices with their start and end apart: 2, of which 2 were waited for; matrix products, arithmetic and copies ran while one was open for 69% of the time, Pallas kernels for 0%

commit v1 on v0

--- a/solution.py
+++ b/solution.py
@@ -1,11 +1,45 @@
+import functools
+import math
+
 import jax
 import jax.numpy as jnp
 from jax import lax
+from jax.experimental import pallas as pl
 from jax.sharding import PartitionSpec as P
 
 BB = 8
 DB = 32
 LANES = 128
+
+
+def dress_rows(rows, b_ac_ref, b_oc_ref, singles_ref, out_ref):
+    singles = singles_ref[...]
+    for row in range(rows):
+        correction = jnp.dot(singles, b_oc_ref[row], preferred_element_type=jnp.float32)
+        slab = b_ac_ref[row].astype(jnp.float32)
+        out_ref[row] = (slab - correction).astype(out_ref.dtype)
+
+
+def dress(b_ac, b_oc, singles):
+    depth, a_width, c_width = b_ac.shape
+    n_occ = b_oc.shape[1]
+    rows = math.gcd(depth, 8)
+    return pl.pallas_call(
+        functools.partial(dress_rows, rows),
+        grid=(depth // rows,),
+        in_specs=[
+            pl.BlockSpec((rows, a_width, c_width), lambda i: (i, 0, 0)),
+            pl.BlockSpec((rows, n_occ, c_width), lambda i: (i, 0, 0)),
+            pl.BlockSpec((a_width, n_occ), lambda i: (0, 0)),
+        ],
+        out_specs=pl.BlockSpec((rows, a_width, c_width), lambda i: (i, 0, 0)),
+        out_shape=jax.ShapeDtypeStruct(b_ac.shape, b_ac.dtype),
+        cost_estimate=pl.CostEstimate(
+            flops=2 * b_ac.size * n_occ,
+            bytes_accessed=4 * b_ac.size + 2 * b_oc.size,
+            transcendentals=0,
+        ),
+    )(b_ac, b_oc, singles)
 
 
 def shards(b_ac, b_oc, t1, f_bd, t2):
@@ -17,8 +51,7 @@
     gathered = lax.all_gather(amplitudes, ("aa", "pb"), axis=0)
     n_aa, n_pb = lax.axis_size("aa"), lax.axis_size("pb")
     gathered = gathered.reshape(n_aa, n_pb, pairs, DB, c_width)
-    correction = jnp.einsum("ka,qkc->qac", t1, b_oc, preferred_element_type=jnp.float32)
-    dressed = (b_ac - correction).astype(jnp.bfloat16)
+    dressed = dress(b_ac, b_oc, t1.T)
     ladder = jnp.einsum("qac,qn->anc", dressed, f_bd, preferred_element_type=jnp.float32)
     ladder = ladder.astype(jnp.bfloat16)
     ladder = ladder.reshape(ladder.shape[0], BB, DB, n_pb, c_width)

time: 368 us -> 365 us (level)
  local copies, waits for them, and re-layouts: 213 us -> 79.8 us
  Pallas kernels: 0 us -> 59.6 us
  matrix products: 93.2 us -> 134 us
  waiting for transfers between devices: 42.8 us -> 74.7 us
    dot_general x1, matrix products: 32.1 us -> 110 us  [shards(): jnp.einsum('qac,qn->anc', dressed, f_bd, preferred_element_type=jnp.float32)]
    convert_element_type x1 -> x0, local copies, waits for them, and re-layouts: 69.6 us -> none  [shards(): dressed = (b_ac - correction).astype(jnp.bfloat16)]
    unnamed x10 -> x8, local copies, waits for them, and re-layouts: 69.1 us -> 5.78 us
    pallas_call x0 -> x1, Pallas kernels: none -> 59.6 us  [dress(): pl.pallas_call(functools.partial(dress_rows, rows), grid=(depth // rows,)...]
    dot_general x1 -> x0, matrix products: 37.5 us -> none  [shards(): jnp.einsum('ka,qkc->qac', t1, b_oc, preferred_element_type=jnp.float32)]
    all_gather x1, waiting for transfers between devices: 2.34 us -> 35.1 us  [shards(): gathered = lax.all_gather(amplitudes, ('aa', 'pb'), axis=0)]
  transfers between devices with their start and end apart: 2 -> 2, of which waited for: 2 -> 2; matrix products, arithmetic and copies ran while one was open for 69% -> 44% of each run, Pallas kernels for 0% -> 17%
where the time goes in v1:
time: 365 us; the launch traced here: 361 us
  matrix products  134 us (37%)
  local copies, waits for them, and re-layouts  79.8 us (22%)
  waiting for transfers between devices  74.7 us (20%)
  Pallas kernels  59.6 us (16%)
  between operations  13.4 us (4%)
    dot_general x1, matrix products, shards(): jnp.einsum('qac,qn->anc', dressed, f_bd, preferred_element_type=jnp.float32)  110 us
    pallas_call x1, Pallas kernels, dress(): pl.pallas_call(functools.partial(dress_rows, rows), grid=(depth // rows,)...  59.6 us
    convert_element_type x1, local copies, waits for them, and re-layouts, shards(): ladder = ladder.astype(jnp.bfloat16)  47.1 us
    reduce_scatter x1, waiting for transfers between devices, shards(): lax.psum_scatter(partial_sums, ('col', 'pb'), scatter_dimension=0, tiled=...  39.6 us
    all_gather x1, waiting for transfers between devices, shards(): gathered = lax.all_gather(amplitudes, ('aa', 'pb'), axis=0)  35.1 us
    all_gather x1, local copies, waits for them, and re-layouts, shards(): gathered = lax.all_gather(amplitudes, ('aa', 'pb'), axis=0)  25.5 us
    dot_general x1, matrix products, shards(): jnp.einsum('xpidc,abdpc->xiab', gathered, ladder, preferred_element_type=...  23.5 us
  transfers between devices with their start and end apart: 2, of which 2 were waited for; matrix products, arithmetic and copies ran while one was open for 44% of the time, Pallas kernels for 17%

profile of v1, /device:TPU:0, one launch (start us, length us, event | category | flops | bytes accessed | tf_op | source)
XLA Modules:
  0.0 361.3 jit_solution(6692746895345035016)
XLA Ops:
  6.5 0.0 copy-start
  6.5 0.0 all-gather.3.cloned.1.call-start
  6.5 2.3 copy.21
  8.9 0.0 all-gather.3.cloned.1.call-update
  8.9 0.0 reduce-scatter.4.cloned.1.call-start
  8.9 1.4 copy.18
  10.3 59.6 %shard_map.55 = bf16[384,128,512]{2,1,0:T(8,128)(2,1)} custom-call(bf16[384,128,512]{2,1,0:T(8,128)(2,1)} %b_ac_ref.1, bf16[384,32,512]{2,1,0:T(8,128)(2,1)} %b_oc_ref.1, bf16[128,32]{1,0:T(8,128)(2,1)} %bitcast.42), custom_call_target="tpu_custom_call" | custom-call | flops 1610612736 | bytes 113246208 | tf_op jit(solution)/shard_map/pallas_call | solution.py:27
  70.0 0.0 copy-done
  70.0 110.2 %convert_bitcast_fusion = bf16[128,256,512]{1,2,0:T(8,128)(2,1)} fusion(bf16[384,128,512]{2,1,0:T(8,128)(2,1)} %shard_map.55, bf16[384,256]{1,0:T(8,128)(2,1)S(1)} %copy-done), kind=kOutput, calls=%fused_computation.2 | convolution fusion | flops 12901679104 | bytes 84082688 | tf_op jit(solution)/shard_map/qac,qn->anc/dot_general | solution.py:55
  180.2 47.1 %copy.20 = bf16[128,256,512]{0,2,1:T(8,128)(2,1)} copy(bf16[128,256,512]{1,2,0:T(8,128)(2,1)} %convert_bitcast_fusion) | data formatting | bytes 67108864 | tf_op jit(solution)/shard_map/convert_element_type | solution.py:56
  227.4 35.1 %all-gather.3.cloned.1.call-done = bf16[2048,32,128]{0,1,2:T(8,128)(2,1)} async-done(((bf16[128,32,128]{0,1,2:T(8,128)(2,1)}), bf16[2048,32,128]{0,1,2:T(8,128)(2,1)}) %all-gather.3.cloned.1.call-update) | async-done | bytes 16777232 | tf_op jit(solution)/shard_map/all_gather | solution.py:51
  262.4 25.5 %copy.22 = bf16[2048,32,128]{2,1,0:T(8,128)(2,1)} copy(bf16[2048,32,128]{0,1,2:T(8,128)(2,1)} %all-gather.3.cloned.1.call-done) | data formatting | bytes 33554432 | tf_op jit(solution)/shard_map/all_gather | solution.py:51
  288.0 0.0 copy-start.1
  288.0 23.5 %fusion.7 = f32[4,128,128,8]{1,2,0,3:T(8,128)S(1)} fusion(bf16[128,8,32,4,128,1]{0,4,3,2,5,1:T(8,128)(2,1)} %bitcast.37, bf16[4,4,128,32,128]{4,3,2,1,0:T(8,128)(2,1)} %bitcast.38), kind=kOutput, calls=%fused_computation.8 | convolution fusion | flops 17179869184 | bytes 52428800 | tf_op jit(solution)/shard_map/xpidc,abdpc->xiab/dot_general | solution.py:58
  311.4 1.4 copy.47
  312.8 0.2 copy.46
  313.0 1.9 copy.31
  314.8 0.0 reduce-scatter.4.cloned.1.call-update
  314.9 39.6 %reduce-scatter.4.cloned.1.call-done = f32[64,1024]{1,0:T(8,128)} async-done(((f32[512,1024]{1,0:T(8,128)}), f32[64,1024]{1,0:T(8,128)}) %reduce-scatter.4.cloned.1.call-update) | async-done | bytes 262160 | tf_op jit(solution)/shard_map/reduce_scatter | solution.py:62
  354.5 0.0 copy-done.1
Async XLA Ops:
  6.5 63.4 %copy-start = (bf16[384,256]{1,0:T(8,128)(2,1)S(1)}, bf16[384,256]{1,0:T(8,128)(2,1)}, u32[]{:S(2)}) copy-start(bf16[384,256]{1,0:T(8,128)(2,1)} %param.8) | copy-start | bytes 589828
  6.5 255.9 %all-gather.3.cloned.1.call-start = ((), (), s32[]{:S(2)}) async-start(), calls=%async_computation.1 | async-start | bytes 17825792 | tf_op jit(solution)/shard_map/all_gather | solution.py:51
  8.9 345.6 %reduce-scatter.4.cloned.1.call-start = ((), (), s32[]{:S(2)}) async-start(), calls=%async_computation.2 | async-start | bytes 2359296 | tf_op jit(solution)/shard_map/reduce_scatter | solution.py:62
  288.0 66.5 %copy-start.1 = (bf16[384,256]{1,0:T(8,128)(2,1)S(1)}, bf16[384,256]{1,0:T(8,128)(2,1)}, u32[]{:S(2)}) copy-start(bf16[384,256]{1,0:T(8,128)(2,1)} %param.8) | copy-start | bytes 589828
Sparse Core Ops, SparseCore 0:
  10.1 252.3 all-gather.2
  315.0 39.4 reduce-scatter.3
